TPU v7x, 256 devices: a whole 4x4x8 slice. The times are simulated.
256 devices in a mesh: row: 8 (over z_hi, core), col: 32 (over z_lo, y, x).
Axes of the slice: x: 4, y: 4, z: 8 (z_hi: 4, z_lo: 2; z = z_hi * 2 + z_lo), core: 2. Of those that a mesh axis runs over, the one named last changes fastest.
Arguments:
- pair_rep: bfloat16 [2048, 2048, 128], P('row', 'col'), may hold values from -6 to 6
- ln_in_gain: float32 [128], replicated, may hold values from 0.1 to 1.9
- ln_in_bias: float32 [128], replicated, may hold values from -3 to 3
- w_left_gate: bfloat16 [128, 128], replicated, may hold values from -0.5 to 0.5
- w_left_proj: bfloat16 [128, 128], replicated, may hold values from -0.5 to 0.5
- w_right_gate: bfloat16 [128, 128], replicated, may hold values from -0.5 to 0.5
- w_right_proj: bfloat16 [128, 128], replicated, may hold values from -0.5 to 0.5
- w_out_gate: bfloat16 [128, 128], replicated, may hold values from -0.5 to 0.5
- ln_out_gain: float32 [128], replicated, may hold values from 0.1 to 1.9
- ln_out_bias: float32 [128], replicated, may hold values from -3 to 3
- w_output: bfloat16 [128, 128], replicated, may hold values from -0.5 to 0.5
Outputs:
- update: bfloat16 [2048, 2048, 128], P('row', 'col')
All inputs are finite; a program needn't handle non-finite values.
Results may differ from a plain program's by a relative error of at most 0.0055.
Values may be sent and summed in bfloat16 or wider, within the bound.
A program may use at most 128 MiB of HBM per device.

v0:
```python
import jax
import jax.numpy as jnp
from jax import lax
from jax.sharding import PartitionSpec as P

KD = 6


def from_root(array, axis, root):
    mine = lax.axis_index(axis) == root
    return lax.psum(jnp.where(mine, array, jnp.zeros_like(array)), axis)


def layer_norm(values, gain, bias):
    mean_val = jnp.mean(values, axis=-1, keepdims=True)
    centred = values - mean_val
    spread = jnp.mean(centred * centred, axis=-1, keepdims=True)
    return centred * lax.rsqrt(spread + 1e-05) * gain + bias


def gated_panel(window, w_gate, w_proj):
    gate_part = jnp.dot(window, w_gate, preferred_element_type=jnp.float32)
    value_part = jnp.dot(window, w_proj, preferred_element_type=jnp.float32)
    return (jax.nn.sigmoid(gate_part) * value_part).astype(jnp.bfloat16)


def body(
    pair_rep,
    ln_in_gain,
    ln_in_bias,
    w_left_gate,
    w_left_proj,
    w_right_gate,
    w_right_proj,
    w_out_gate,
    ln_out_gain,
    ln_out_bias,
    w_output,
):
    tile_rows, tile_cols, channels = pair_rep.shape
    normed = layer_norm(pair_rep.astype(jnp.float32), ln_in_gain, ln_in_bias).astype(jnp.bfloat16)
    window = normed[:, :KD, :]
    left_local = gated_panel(window, w_left_gate, w_left_proj)
    right_local = gated_panel(window, w_right_gate, w_right_proj)
    right_all = lax.all_gather(right_local, "col", axis=1, tiled=True)
    col_index = lax.axis_index("col")
    row_index = lax.axis_index("row")
    offset = jnp.clip(col_index * tile_cols - row_index * tile_rows, 0, tile_rows - tile_cols)
    picked = lax.dynamic_slice_in_dim(right_all, offset, tile_cols, 0)
    source_row = col_index * tile_cols // tile_rows
    right_panel = from_root(picked, "row", source_row)
    left_panel = lax.all_gather(left_local, "col", axis=1, tiled=True)
    product = jnp.einsum(
        "ikc,jkc->ijc", left_panel, right_panel, preferred_element_type=jnp.float32
    )
    mixed = layer_norm(product, ln_out_gain, ln_out_bias).astype(jnp.bfloat16)
    gate = jax.nn.sigmoid(jnp.dot(normed, w_out_gate, preferred_element_type=jnp.float32))
    projected = jnp.dot(mixed, w_output, preferred_element_type=jnp.float32)
    return (gate * projected).astype(jnp.bfloat16)


def solution(mesh):
    in_specs = (P("row", "col", None), P(), P(), P(), P(), P(), P(), P(), P(), P(), P())
    out_specs = P("row", "col", None)
    return jax.shard_map(body, mesh=mesh, in_specs=in_specs, out_specs=out_specs, check_vma=False)
```

profile of v0, /device:TPU:37, one launch (start us, length us, event | category | flops | bytes accessed | tf_op | source)
XLA Modules:
  0.0 545.8 jit_solution(5550931189147480396)
XLA Ops:
  6.5 0.0 all-gather.3.cloned.1.call-start
  6.6 0.0 copy-start.1
  6.6 10.7 %convert_reduce_fusion = f32[256,64]{0,1:T(8,128)S(1)} fusion(bf16[256,64,128]{2,1,0:T(8,128)(2,1)} %param.11), kind=kLoop, calls=%fused_computation.1 | loop fusion | flops 4177920 | bytes 4259840 | tf_op jit(solution)/shard_map/reduce_sum | solution.py:15
  17.3 0.0 copy-start.4
  17.3 6.1 %fusion.2 = f32[256,64]{0,1:T(8,128)S(1)} fusion(f32[256,64]{0,1:T(8,128)S(1)} %broadcast_multiply_fusion.1, bf16[256,64,128]{2,1,0:T(8,128)(2,1)} %param.11), kind=kLoop, calls=%fused_computation.4 | loop fusion | flops 8372224 | bytes 4325376 | tf_op jit(solution)/shard_map/reduce_sum | solution.py:17
  23.5 0.0 copy-start.5
  23.5 9.3 %fusion.5 = bf16[256,64,128]{2,0,1:T(8,128)(2,1)S(1)} fusion(f32[128]{0:T(128)S(1)} %copy-done.6, f32[128]{0:T(128)S(1)} %copy-done.7, f32[256,64]{0,1:T(8,128)S(1)} %add_rsqrt_fusion.1, f32[256,64]{0,1:T(8,128)S(1)} %broadcast_multiply_fusion.1, bf16[256,64,128]{2,1,0:T(8,128)(2,1)S(1)} %copy-done.1), kind=kLoop, calls=%fused_computation.7 | loop fusion | flops 12582912 | bytes 8520704 | tf_op jit(solution)/shard_map/convert_element_type | solution.py:41
  32.8 0.4 fusion.13
  33.1 1.6 copy-done.2
  34.7 1.0 fusion.14
  35.7 0.0 all-gather.3.cloned.1.call-update
  35.8 0.2 all-gather.5.cloned.1.call-start
  36.0 1.3 fusion.10
  37.4 2.0 fusion.15
  39.4 0.0 all-gather.5.cloned.1.call-update
  39.4 0.0 all-reduce.2.cloned.1.call-start
  39.5 156.4 %all-gather.3.cloned.1.call-done = bf16[256,192,128]{2,0,1:T(8,128)(2,1)} async-done(((bf16[256,6,128]{2,0,1:T(8,128)(2,1)}), bf16[256,192,128]{2,0,1:T(8,128)(2,1)}) %all-gather.3.cloned.1.call-update) | async-done | bytes 12582928 | tf_op jit(solution)/shard_map/all_gather | solution.py:45
  195.9 3.6 constant_dynamic-slice_fusion
  199.5 8.0 %copy.49 = bf16[64,192,128]{1,0,2:T(8,128)(2,1)} copy(bf16[64,192,128]{2,0,1:T(8,128)(2,1)S(1)} %constant_dynamic-slice_fusion) | data formatting | bytes 6291456
  207.4 2.3 broadcast_select_fusion
  209.7 0.0 all-reduce.2.cloned.1.call-update
  209.8 164.2 %all-gather.5.cloned.1.call-done = bf16[256,192,128]{2,0,1:T(8,128)(2,1)} async-done(((bf16[256,6,128]{2,0,1:T(8,128)(2,1)}), bf16[256,192,128]{2,0,1:T(8,128)(2,1)}) %all-gather.5.cloned.1.call-update) | async-done | bytes 12582928 | tf_op jit(solution)/shard_map/all_gather | solution.py:52
  373.9 16.5 %copy.44 = bf16[256,192,128]{0,1,2:T(8,128)(2,1)} copy(bf16[256,192,128]{2,0,1:T(8,128)(2,1)} %all-gather.5.cloned.1.call-done) | data formatting | bytes 25165824 | tf_op jit(solution)/shard_map/all_gather | solution.py:52
  390.4 125.4 %all-reduce.2.cloned.1.call-done = bf16[64,192,128]{1,0,2:T(8,128)(2,1)} async-done(((bf16[64,192,128]{1,0,2:T(8,128)(2,1)}), bf16[64,192,128]{1,0,2:T(8,128)(2,1)}) %all-reduce.2.cloned.1.call-update) | async-done | bytes 3145744 | tf_op jit(solution)/shard_map/psum | solution.py:11
  515.8 8.3 %bitcast_reduce_fusion = (f32[256,64]{0,1:T(8,128)S(1)}, f32[128,64,256]{2,1,0:T(8,128)S(1)}) fusion(bf16[64,192,128]{1,0,2:T(8,128)(2,1)} %all-reduce.2.cloned.1.call-done, bf16[256,192,128]{0,1,2:T(8,128)(2,1)} %copy.44), kind=kOutput, calls=%fused_computation.9 | convolution fusion | flops 807387136 | bytes 24182784 | tf_op jit(solution)/shard_map/ikc,jkc->ijc/dot_general | solution.py:53
  524.2 0.0 copy-start.8
  524.2 0.0 copy-start.9
  524.2 0.9 multiply_reduce_fusion
  525.1 1.6 add_convert_fusion
  526.8 4.9 fusion.6
  531.7 2.8 multiply_convert_fusion
  534.5 4.7 copy.46
  (24 shorter events, 0.1 us)
Async XLA Ops:
  6.5 520.2 %copy-start = (bf16[128,128]{1,0:T(8,128)(2,1)S(1)}, bf16[128,128]{1,0:T(8,128)(2,1)}, u32[]{:S(2)}) copy-start(bf16[128,128]{1,0:T(8,128)(2,1)} %param.21) | copy-start | bytes 98308
  6.5 16.9 %copy-start.6 = (f32[128]{0:T(128)S(1)}, f32[128]{0:T(128)}, u32[]{:S(2)}) copy-start(f32[128]{0:T(128)} %param.13) | copy-start | bytes 1540
  6.5 16.9 %copy-start.7 = (f32[128]{0:T(128)S(1)}, f32[128]{0:T(128)}, u32[]{:S(2)}) copy-start(f32[128]{0:T(128)} %param.12) | copy-start | bytes 1540
  6.5 26.2 %copy-start.10 = (bf16[128,128]{1,0:T(8,128)(2,1)S(1)}, bf16[128,128]{1,0:T(8,128)(2,1)}, u32[]{:S(2)}) copy-start(bf16[128,128]{1,0:T(8,128)(2,1)} %param.16) | copy-start | bytes 98308
  6.5 189.3 %all-gather.3.cloned.1.call-start = ((), (), s32[]{:S(2)}) async-start(), calls=%async_computation | async-start | bytes 12976128 | tf_op jit(solution)/shard_map/all_gather | solution.py:45
  6.6 16.9 %copy-start.1 = (bf16[256,64,128]{2,1,0:T(8,128)(2,1)S(1)}, bf16[256,64,128]{2,1,0:T(8,128)(2,1)}, u32[]{:S(2)}) copy-start(bf16[256,64,128]{2,1,0:T(8,128)(2,1)} %param.11) | copy-start | bytes 12582916
  17.3 17.5 %copy-start.4 = (bf16[128,128]{1,0:T(8,128)(2,1)S(1)}, bf16[128,128]{1,0:T(8,128)(2,1)}, u32[]{:S(2)}) copy-start(bf16[128,128]{1,0:T(8,128)(2,1)} %param.17) | copy-start | bytes 98308
  17.3 18.7 %copy-start.11 = (bf16[128,128]{1,0:T(8,128)(2,1)S(1)}, bf16[128,128]{1,0:T(8,128)(2,1)}, u32[]{:S(2)}) copy-start(bf16[128,128]{1,0:T(8,128)(2,1)} %param.14) | copy-start | bytes 98308
  23.5 13.9 %copy-start.5 = (bf16[128,128]{1,0:T(8,128)(2,1)S(1)}, bf16[128,128]{1,0:T(8,128)(2,1)}, u32[]{:S(2)}) copy-start(bf16[128,128]{1,0:T(8,128)(2,1)} %param.15) | copy-start | bytes 98308
  32.8 2.0 copy-start.2
  35.8 338.2 %all-gather.5.cloned.1.call-start = ((), (), s32[]{:S(2)}) async-start(), calls=%async_computation.2 | async-start | bytes 12976128 | tf_op jit(solution)/shard_map/all_gather | solution.py:52
  39.4 476.4 %all-reduce.2.cloned.1.call-start = ((), (), s32[]{:S(2)}) async-start(), calls=%async_computation.1 | async-start | bytes 8388608 | tf_op jit(solution)/shard_map/psum | solution.py:11
  524.2 0.9 copy-start.8
  524.2 0.9 copy-start.9
  526.8 4.9 copy-start.3
  526.8 4.9 copy-start.12
Sparse Core Ops, SparseCore 0:
  35.9 159.9 all-gather.2
  197.6 176.2 all-gather.4
  376.6 139.1 all-reduce.1
where the time goes:
time: 549 us; the launch traced here: 546 us
  waiting for transfers between devices  446 us (81%)
  local copies, waits for them, and re-layouts  34.5 us (6%)
  other arithmetic  30.9 us (6%)
  matrix products  20.8 us (4%)
  between operations  13.4 us (2%)
    all_gather x1, waiting for transfers between devices, body(): left_panel = lax.all_gather(left_local, 'col', axis=1, tiled=True)  164 us
    all_gather x1, waiting for transfers between devices, body(): right_all = lax.all_gather(right_local, 'col', axis=1, tiled=True)  156 us
    psum x1, waiting for transfers between devices, from_root(): return lax.psum(jnp.where(mine, array, jnp.zeros_like(array)), axis)  125 us
    all_gather x1, local copies, waits for them, and re-layouts, body(): left_panel = lax.all_gather(left_local, 'col', axis=1, tiled=True)  16.5 us
  transfers between devices with their start and end apart: 3, of which 3 were waited for; matrix products, arithmetic and copies ran while one was open for 6% of the time, Pallas kernels for 0%

commit v1 on v0

v1 whole, which is shorter than its diff:
```python
import functools

import jax
import jax.numpy as jnp
from jax import lax
from jax.experimental import pallas as pl
from jax.experimental.pallas import tpu as pltpu
from jax.sharding import PartitionSpec as P

MESH = pl.DeviceIdType.MESH
F32 = jnp.float32
BF16 = jnp.bfloat16
NK = 6
DF = (0, -1, 1, 2)
N_COPIES = 84


def norm_rows(x, gain, bias):
    average = jnp.full((128, 128), 1.0 / 128, BF16)
    centred = x.astype(F32) - jnp.dot(x, average, preferred_element_type=F32)
    spread = jnp.dot((centred * centred).astype(BF16), average, preferred_element_type=F32)
    return (centred * lax.rsqrt(spread + 1e-05) * gain + bias).astype(BF16)


def kernel(
    z_hbm, gin_ref, bin_ref, wlg_ref, wlp_ref, wrg_ref, wrp_ref, wog_ref, gout_ref, bout_ref, wo_ref,
    out_hbm,
    zv, zf, wt, normed_w, panel, r_send, r_gather, r_nat, r_mat, lefts, swap, acc, proj, gain_c, bias_c,
    z_sem, out_sem, send_sem, recv_sem, r1_send, r1_recv, r2_send, r2_recv, rf_send, rf_recv, r3_send, r3_recv,
):
    row, col = lax.axis_index("row"), lax.axis_index("col")
    zh, core = row // 2, row % 2
    zl, y, x = col // 16, (col // 4) % 4, col % 4

    def dev(zh_=None, core_=None, zl_=None, y_=None, x_=None):
        a = zh if zh_ is None else zh_
        b = core if core_ is None else core_
        c = zl if zl_ is None else zl_
        d = y if y_ is None else y_
        e = x if x_ is None else x_
        return (a * 2 + b, c * 16 + d * 4 + e)

    barrier = pltpu.get_barrier_semaphore()

    def greet(target):
        pl.semaphore_signal(barrier, inc=1, device_id=target, device_id_type=MESH)

    for n in range(1, 16):
        p = (y * 4 + x + n) % 16
        greet(dev(y_=p // 4, x_=p % 4))
    for n in range(1, 8):
        p = (zh * 2 + zl + n) % 8
        greet(dev(zh_=p // 2, zl_=p % 2))
    greet(dev(core_=1 - core))

    head = pltpu.make_async_copy(z_hbm.at[:, pl.ds(0, 16), :], zv.at[:, pl.ds(0, 16), :], z_sem.at[0])
    rest = pltpu.make_async_copy(z_hbm.at[:, pl.ds(16, 48), :], zv.at[:, pl.ds(16, 48), :], z_sem.at[1])
    head.start()
    rest.start()

    gin, bias_in = gin_ref[...].reshape(1, 128), bin_ref[...].reshape(1, 128)
    for n, w in enumerate((wlg_ref, wlp_ref, wrg_ref, wrp_ref)):
        wt[n * 128 : (n + 1) * 128, :] = w[...].astype(F32).T.astype(BF16)
    gain_c[...] = jnp.broadcast_to(gout_ref[...].reshape(1, 128), (128, 128)).T
    bias_c[...] = jnp.broadcast_to(bout_ref[...].reshape(1, 128), (128, 128)).T

    head.wait()

    def widen(b, _):
        i0 = pl.multiple_of(b * 8, 8)
        v = zv[pl.ds(i0, 8), 0:16, :].astype(F32)
        for i in range(8):
            zf[pl.ds((i0 + i) * 9, 8), :] = v[i, 0:8]
        return 0

    lax.fori_loop(0, 32, widen, 0, unroll=4)

    def norm_window(k, _):
        v = zf[pl.ds(k, 256, stride=9), :].astype(BF16)
        normed_w[k] = norm_rows(v, gin, bias_in)
        return 0

    lax.fori_loop(0, NK, norm_window, 0, unroll=3)

    def project(k, part):
        return lax.dot_general(
            wt[part * 256 : part * 256 + 256, :], normed_w[k], (((1,), (1,)), ((), ())), preferred_element_type=F32
        )

    def window_left(k, _):
        both = project(k, 0)
        left = (jax.nn.sigmoid(both[0:128]) * both[128:256]).astype(BF16)
        for h in range(2):
            for ab in range(2):
                pair = (y * 4 + x) if ab == 0 else (x * 4 + y)
                panel[h, ab, pair, zl * NK + k] = left[ab * 64 : ab * 64 + 64, h * 128 : h * 128 + 128]
        return 0

    low = lax.broadcasted_iota(jnp.int32, (32, 128), 1) < 64

    def window_right(k, _):
        both = project(k, 1)
        right = jax.nn.sigmoid(both[0:128]) * both[128:256]
        for u in range(2):
            for ab in range(2):
                lo = right[ab * 64 : ab * 64 + 32, u * 128 : u * 128 + 128]
                hi = right[ab * 64 + 32 : ab * 64 + 64, u * 128 : u * 128 + 128]
                r_send[2 * u, k, ab * 32 : ab * 32 + 32, :] = jnp.where(low, lo, pltpu.roll(hi, 64, 1)).astype(BF16)
                r_send[2 * u + 1, k, ab * 32 : ab * 32 + 32, :] = jnp.where(low, pltpu.roll(lo, 64, 1), hi).astype(BF16)
        return 0

    lax.fori_loop(0, NK, window_right, 0, unroll=3)
    pl.semaphore_wait(barrier, 23)

    count = [0]
    copies = {}

    def left_copy(name, ref, target):
        n = count[0]
        count[0] += 1
        c = pltpu.make_async_remote_copy(
            src_ref=ref, dst_ref=ref, send_sem=send_sem.at[n], recv_sem=recv_sem.at[n], device_id=target, device_id_type=MESH
        )
        c.start()
        copies[name] = (n, c)

    def arrived(name, ref):
        n, _ = copies[name]
        pltpu.make_async_copy(ref, ref, recv_sem.at[n]).wait()

    def first(ab):
        return x if ab == 0 else y

    def second(ab):
        return y if ab == 0 else x

    def step_first(ab, d):
        return dev(x_=(x + d) % 4) if ab == 0 else dev(y_=(y + d) % 4)

    def step_second(ab, d):
        return dev(y_=(y + d) % 4) if ab == 0 else dev(x_=(x + d) % 4)

    def pair_ref(h, ab, ds, df, half=None):
        p = ((second(ab) + ds) % 4) * 4 + (first(ab) + df) % 4
        if half is None:
            return panel.at[h, ab, p]
        return panel.at[h, ab, p, :, pl.ds(half * 32, 32), :]

    def z_ref(h, ab, z):
        return panel.at[h, ab, second(ab) * 4 + first(ab), pl.ds(z * NK, NK)]

    def send_z(h):
        for ab in range(2):
            left_copy(("z", h, ab), z_ref(h, ab, zl), dev(zl_=1 - zl))

    def wait_z(h):
        for ab in range(2):
            arrived(("z", h, ab), z_ref(h, ab, 1 - zl))

    def send_p1(h):
        for ab in range(2):
            for d in (1, -1):
                left_copy(("p1", h, ab, d), pair_ref(h, ab, 0, 0), step_first(ab, d))

    def send_q1(h, df):
        for ab in range(2):
            for d in (1, -1):
                left_copy(("q1", h, ab, df, d), pair_ref(h, ab, 0, df), step_second(ab, d))

    def pass_p1(h):
        for d in (1, -1):
            for ab in range(2):
                arrived(("p1", h, ab, d), pair_ref(h, ab, 0, -d))
                half = 0 if d == 1 else 1
                left_copy(("p2", h, ab, d), pair_ref(h, ab, 0, -d, half), step_first(ab, d))

    def wait_p2(h):
        for d in (1, -1):
            for ab in range(2):
                half = 0 if d == 1 else 1
                arrived(("p2", h, ab, d), pair_ref(h, ab, 0, 2, half))

    def pass_q1(h, df):
        for d in (1, -1):
            for ab in range(2):
                arrived(("q1", h, ab, df, d), pair_ref(h, ab, -d, df))
                half = 0 if d == 1 else 1
                left_copy(("q2", h, ab, df, d), pair_ref(h, ab, -d, df, half), step_second(ab, d))

    def wait_q2(h, df):
        for d in (1, -1):
            for ab in range(2):
                half = 0 if d == 1 else 1
                arrived(("q2", h, ab, df, d), pair_ref(h, ab, 2, df, half))

    own_slot = y * 4 + x
    ty = row % 4
    gathers = jnp.logical_and(y // 2 == zh % 2, core == y % 2)
    relays = core == y % 2

    def r1_ref(ref, n, ab):
        return ref.at[n, :, pl.ds(ab * 32, 32), :]

    def r1_copy(q, ab):
        return pltpu.make_async_remote_copy(
            src_ref=r1_ref(r_send, q, ab), dst_ref=r1_ref(r_gather, own_slot, ab),
            send_sem=r1_send.at[q * 2 + ab], recv_sem=r1_recv.at[ab], device_id=dev(y_=ty, x_=q), device_id_type=MESH,
        )

    def r1_mine(q):
        return jnp.logical_and(ty == y, x == q)

    def start_r1():
        for ab in range(2):
            for q in range(4):
                @pl.when(r1_mine(q))
                def _():
                    pltpu.make_async_copy(r1_ref(r_send, q, ab), r1_ref(r_gather, own_slot, ab), r1_recv.at[ab]).start()

                @pl.when(jnp.logical_not(r1_mine(q)))
                def _():
                    r1_copy(q, ab).start()

    def piece(ref, p):
        return ref.at[:, :, pl.ds(p * 16, 16), :]

    def r2_copy(p, o):
        return pltpu.make_async_remote_copy(
            src_ref=piece(r_gather, p), dst_ref=piece(r_nat.at[zl], p), send_sem=r2_send.at[p * 4 + o],
            recv_sem=r2_recv.at[p * 2 + zl], device_id=dev(zh_=(zh + o) % 4, zl_=zh // 2), device_id_type=MESH,
        )

    at_home = zl == zh // 2

    def start_r2(ab):
        @pl.when(gathers)
        def _():
            got = r_gather.at[:, :, pl.ds(ab * 32, 32), :]
            pltpu.make_async_copy(got, got, r1_recv.at[ab]).wait()
            for p in (2 * ab, 2 * ab + 1):
                r2_copy(p, 1).start()
                r2_copy(p, 3).start()

                @pl.when(at_home)
                def _():
                    pltpu.make_async_copy(piece(r_gather, p), piece(r_nat.at[zl], p), r2_recv.at[p * 2 + zl]).start()

                @pl.when(jnp.logical_not(at_home))
                def _():
                    r2_copy(p, 0).start()

    rel = (zh + 4 - (2 * zl + y // 2)) % 4

    def far_ref(p, z, half):
        return r_nat.at[z, pl.ds(half * 8, 8), :, pl.ds(p * 16, 16), :]

    def far_copy(p, z, half):
        return pltpu.make_async_remote_copy(
            src_ref=far_ref(p, z, half), dst_ref=far_ref(p, z, half), send_sem=rf_send.at[p * 2 + z],
            recv_sem=rf_recv.at[p * 4 + z * 2 + half],
            device_id=dev(zh_=(zh + (1 if half == 0 else 3)) % 4), device_id_type=MESH,
        )

    def r3_copy(p, z):
        part = piece(r_nat.at[z], p)
        return pltpu.make_async_remote_copy(
            src_ref=part, dst_ref=part, send_sem=r3_send.at[p * 2 + z], recv_sem=r3_recv.at[p * 2 + z],
            device_id=dev(core_=1 - core), device_id_type=MESH,
        )

    def pass_r2(p):
        @pl.when(jnp.logical_and(relays, rel != 2))
        def _():
            for z in range(2):
                part = piece(r_nat.at[z], p)
                pltpu.make_async_copy(part, part, r2_recv.at[p * 2 + z]).wait()
                for half in range(2):
                    @pl.when(rel == 1 + 2 * half)
                    def _():
                        far_copy(p, z, half).start()
                r3_copy(p, z).start()

    def wait_right(p):
        @pl.when(jnp.logical_and(relays, rel == 2))
        def _():
            for z in range(2):
                for half in range(2):
                    part = far_ref(p, z, half)
                    pltpu.make_async_copy(part, part, rf_recv.at[p * 4 + z * 2 + half]).wait()
                r3_copy(p, z).start()

        @pl.when(jnp.logical_not(relays))
        def _():
            for z in range(2):
                part = piece(r_nat.at[z], p)
                pltpu.make_async_copy(part, part, r3_recv.at[p * 2 + z]).wait()

    def gate_part(lo, hi):
        def body(b, _):
            i0 = pl.multiple_of(b * 4, 4)
            normed = norm_rows(zv[pl.ds(i0, 4)].reshape(256, 128), gin, bias_in)
            g = jax.nn.sigmoid(jnp.dot(normed, wog_ref[...], preferred_element_type=F32))
            zv[pl.ds(i0, 4)] = g.astype(BF16).reshape(4, 64, 128)
            return 0

        lax.fori_loop(lo, hi, body, 0, unroll=4)

    def prep_right(p):
        ab = p // 2

        def relay(s, _):
            for f in range(4):
                slot_ = (s * 4 + f) if ab == 0 else (f * 4 + s)
                for z in range(2):
                    for k in range(NK):
                        zf[pl.ds(s * 48 + f * 12 + z * NK + k, 16, stride=193), :] = r_nat[
                            z, slot_, k, p * 16 : p * 16 + 16, :
                        ].astype(F32)
            return 0

        lax.fori_loop(0, 4, relay, 0)

        def turn(c, _):
            m = zf[pl.ds(c * 193, 192), :]
            r_mat[p * 16 + c] = m.astype(BF16).T
            return 0

        lax.fori_loop(0, 16, turn, 0, unroll=4)

    def relayout(h, ds):
        for ab in range(2):
            s = (second(ab) + ds) % 4

            def relay(f, _):
                for k in range(2 * NK):
                    rows = pl.ds(f * 12 + k, 64, stride=49)
                    swap[ab, rows, :] = panel[h, ab, s * 4 + f, k].astype(F32)
                return 0

            lax.fori_loop(0, 4, relay, 0)

            def pack(c, _):
                v = swap[ab, pl.ds(c * 49, 48), :]
                lefts[h, ab * 64 + c, pl.ds(pl.multiple_of(s * 48, 16), 48), :] = v.astype(BF16)
                return 0

            lax.fori_loop(0, 64, pack, 0, unroll=8)

    def multiply(h, p):
        def mul(n, _):
            c2 = p * 16 + n
            for cp in range(2):
                c = (p // 2) * 64 + cp * 32 + (p % 2) * 16 + n
                part = jnp.dot(r_mat[c2, cp * 64 : cp * 64 + 64, :], lefts[h, c], preferred_element_type=F32)
                acc[pl.ds(c * 65, 64), :] = part
            return 0

        lax.fori_loop(0, 16, mul, 0, unroll=4)

    def finish(h):
        def column(j, _):
            p = acc[pl.ds(j, 128, stride=65), :]
            mean = jnp.mean(p, axis=0, keepdims=True)
            centred = p - mean
            spread = jnp.mean(centred * centred, axis=0, keepdims=True)
            mixed = centred * lax.rsqrt(spread + 1e-05) * gain_c[...] + bias_c[...]
            turned = mixed.astype(BF16).T
            proj[pl.ds(j, 128, stride=65), :] = jnp.dot(turned, wo_ref[...], preferred_element_type=F32)
            return 0

        lax.fori_loop(0, 64, column, 0, unroll=4)

        for part in range(4):
            def body(i, _):
                g = zv[h * 128 + i].astype(F32)
                v = g * proj[pl.ds(i * 65, 64), :]
                zv[h * 128 + i] = v.astype(BF16)
                return 0

            lax.fori_loop(part * 32, part * 32 + 32, body, 0, unroll=8)
            out_copy(h, part).start()

    def out_copy(h, part):
        rows = pl.ds(h * 128 + part * 32, 32)
        return pltpu.make_async_copy(zv.at[rows], out_hbm.at[rows], out_sem.at[h * 4 + part])

    start_r1()
    lax.fori_loop(0, NK, window_left, 0, unroll=3)
    send_z(0)
    send_z(1)
    rest.wait()
    gate_part(0, 4)
    wait_z(0)
    send_p1(0)
    send_q1(0, 0)
    gate_part(4, 8)
    start_r2(0)
    gate_part(8, 12)
    pass_p1(0)
    send_q1(0, -1)
    send_q1(0, 1)
    start_r2(1)
    gate_part(12, 20)
    pass_q1(0, 0)
    wait_p2(0)
    send_q1(0, 2)
    gate_part(20, 28)
    wait_z(1)
    send_p1(1)
    relayout(0, 0)
    gate_part(28, 36)
    pass_q1(0, -1)
    pass_q1(0, 1)
    send_q1(1, 0)
    gate_part(36, 44)
    pass_r2(0)
    gate_part(44, 48)
    pass_q1(0, 2)
    pass_p1(1)
    send_q1(1, -1)
    send_q1(1, 1)
    gate_part(48, 56)
    pass_r2(1)
    gate_part(56, 64)
    relayout(0, -1)
    pass_q1(1, 0)
    wait_p2(1)
    send_q1(1, 2)
    pass_r2(2)
    relayout(0, 1)
    for df in DF:
        wait_q2(0, df)
    relayout(0, 2)
    pass_r2(3)
    pass_q1(1, -1)
    pass_q1(1, 1)
    wait_right(0)
    prep_right(0)
    multiply(0, 0)
    wait_right(1)
    prep_right(1)
    multiply(0, 1)
    relayout(1, 0)
    wait_right(2)
    prep_right(2)
    multiply(0, 2)
    pass_q1(1, 2)
    wait_right(3)
    prep_right(3)
    multiply(0, 3)
    finish(0)
    relayout(1, -1)
    relayout(1, 1)
    for df in DF:
        wait_q2(1, df)
    relayout(1, 2)
    for p in range(4):
        multiply(1, p)
    finish(1)

    for n, c in copies.values():
        c.wait_send()
    for q in range(4):
        @pl.when(jnp.logical_not(r1_mine(q)))
        def _():
            for ab in range(2):
                r1_copy(q, ab).wait_send()

    @pl.when(gathers)
    def _():
        for p in range(4):
            r2_copy(p, 1).wait_send()
            r2_copy(p, 3).wait_send()

        @pl.when(jnp.logical_not(at_home))
        def _():
            for p in range(4):
                r2_copy(p, 0).wait_send()

    @pl.when(relays)
    def _():
        for p in range(4):
            for z in range(2):
                for half in range(2):
                    @pl.when(rel == 1 + 2 * half)
                    def _():
                        far_copy(p, z, half).wait_send()
                r3_copy(p, z).wait_send()

    for h in range(2):
        for part in range(4):
            out_copy(h, part).wait()


def body(*args):
    vmem = pl.BlockSpec(memory_space=pltpu.VMEM)
    anywhere = pl.BlockSpec(memory_space=pl.ANY)
    return pl.pallas_call(
        kernel,
        out_shape=jax.ShapeDtypeStruct((256, 64, 128), BF16),
        in_specs=[anywhere] + [vmem] * 10,
        out_specs=anywhere,
        scratch_shapes=[
            pltpu.VMEM((256, 64, 128), BF16),
            pltpu.VMEM((3104, 128), F32),
            pltpu.VMEM((512, 128), BF16),
            pltpu.VMEM((NK, 256, 128), BF16),
            pltpu.VMEM((2, 2, 16, 12, 64, 128), BF16),
            pltpu.VMEM((4, NK, 64, 128), BF16),
            pltpu.VMEM((16, NK, 64, 128), BF16),
            pltpu.VMEM((2, 16, NK, 64, 128), BF16),
            pltpu.VMEM((64, 128, 192), BF16),
            pltpu.VMEM((2, 128, 192, 128), BF16),
            pltpu.VMEM((2, 64 * 49, 128), F32),
            pltpu.VMEM((128 * 65, 128), F32),
            pltpu.VMEM((128 * 65, 128), F32),
            pltpu.VMEM((128, 128), F32),
            pltpu.VMEM((128, 128), F32),
            pltpu.SemaphoreType.DMA((2,)),
            pltpu.SemaphoreType.DMA((8,)),
            pltpu.SemaphoreType.DMA((N_COPIES,)),
            pltpu.SemaphoreType.DMA((N_COPIES,)),
            pltpu.SemaphoreType.DMA((8,)),
            pltpu.SemaphoreType.DMA((2,)),
            pltpu.SemaphoreType.DMA((16,)),
            pltpu.SemaphoreType.DMA((8,)),
            pltpu.SemaphoreType.DMA((8,)),
            pltpu.SemaphoreType.DMA((16,)),
            pltpu.SemaphoreType.DMA((8,)),
            pltpu.SemaphoreType.DMA((8,)),
        ],
        compiler_params=pltpu.CompilerParams(
            collective_id=0, has_side_effects=True, vmem_limit_bytes=60 * 1024 * 1024
        ),
        cost_estimate=pl.CostEstimate(flops=2_000_000_000, bytes_accessed=8_400_000, transcendentals=2_000_000),
    )(*args)


def solution(mesh):
    in_specs = (P("row", "col", None),) + (P(),) * 10
    return jax.shard_map(body, mesh=mesh, in_specs=in_specs, out_specs=P("row", "col", None), check_vma=False)
```

time: 549 us -> 110 us (0.20)
  waiting for transfers between devices: 446 us -> 0 us
  Pallas kernels: 0 us -> 105 us
  other arithmetic: 30.9 us -> 0 us
  local copies, waits for them, and re-layouts: 34.5 us -> 5.16 us
  matrix products: 20.8 us -> 0 us
  between operations: 13.4 us -> 0.01 us
    all_gather x2 -> x0, waiting for transfers between devices: 321 us -> none  [the longest x1 164 us: body(): left_panel = lax.all_gather(left_local, 'col', axis=1, tiled=True)]
    psum x1 -> x0, waiting for transfers between devices: 125 us -> none  [from_root(): return lax.psum(jnp.where(mine, array, jnp.zeros_like(array)), axis)]
    pallas_call x0 -> x1, Pallas kernels: none -> 105 us  [body(): pl.pallas_call(kernel, out_shape=jax.ShapeDtypeStruct((256, 64, 128), BF1...]
    dot_general x7 -> x0, matrix products: 20.8 us -> none  [the longest x1 8.34 us: body(): jnp.einsum('ikc,jkc->ijc', left_panel, right_panel, preferred_element_typ...]
    reduce_sum x3 -> x0, other arithmetic: 17.6 us -> none  [the longest x1 10.7 us: layer_norm(): mean_val = jnp.mean(values, axis=-1, keepdims=True)]
    all_gather x1 -> x0, local copies, waits for them, and re-layouts: 16.5 us -> none  [body(): left_panel = lax.all_gather(left_local, 'col', axis=1, tiled=True)]
    convert_element_type x2 -> x0, other arithmetic: 10.9 us -> none  [the longest x1 9.28 us: body(): layer_norm(pair_rep.astype(jnp.float32), ln_in_gain, ln_in_bias)]
  transfers between devices with their start and end apart: 3 -> 0, of which waited for: 3 -> 0; matrix products, arithmetic and copies ran while one was open for 6% -> 0% of each run, Pallas kernels for 0% -> 0%
where the time goes in v1:
time: 110 us
  Pallas kernels  105 us (95%)
  local copies, waits for them, and re-layouts  5.16 us (5%)
    pallas_call x1, Pallas kernels, body(): pl.pallas_call(kernel, out_shape=jax.ShapeDtypeStruct((256, 64, 128), BF1...  105 us
    unnamed x1, local copies, waits for them, and re-layouts  5.16 us

profile of v1, /device:TPU:37, one launch (start us, length us, event | category | flops | bytes accessed | tf_op | source)
XLA Modules:
  0.0 110.2 jit_solution(13772538463021139599)
XLA Ops:
  0.0 105.0 %shard_map.109 = bf16[256,64,128]{2,1,0:T(8,128)(2,1)} custom-call(bf16[256,64,128]{2,1,0:T(8,128)(2,1)} %z_hbm.1, f32[128]{0:T(128)} %gin_ref.1, f32[128]{0:T(128)} %bin_ref.1, bf16[128,128]{1,0:T(8,128)(2,1)} %wlg_ref.1, bf16[128,128]{1,0:T(8,128)(2,1)} %wlp_ref.1, bf16[128,128]{1,0:T(8,128)(2,1)} %wrg_ref.1, bf16[128,128]{1,0:T(8,128)(2,1)} %wrp_ref.1, ...), custom_call_target="tpu_custom_call" | custom-call | flops 2000000000 | bytes 8400000 | tf_op jit(solution)/shard_map/pallas_call | solution.py:498
  105.1 5.2 %copy.13 = bf16[256,64,128]{2,1,0:T(8,128)(2,1)} copy(bf16[256,64,128]{2,1,0:T(8,128)(2,1)} %shard_map.109) | data formatting | bytes 8388608

commit v2 on v1

--- a/solution.py
+++ b/solution.py
@@ -25,7 +25,7 @@
 def kernel(
     z_hbm, gin_ref, bin_ref, wlg_ref, wlp_ref, wrg_ref, wrp_ref, wog_ref, gout_ref, bout_ref, wo_ref,
     out_hbm,
-    zv, zf, wt, normed_w, panel, r_send, r_gather, r_nat, r_mat, lefts, swap, acc, proj, gain_c, bias_c,
+    zv, zf, wt, normed_w, panel, r_send, r_gather, r_nat, r_mat, lefts, swap, acc, sums, proj, gain_c, bias_c,
     z_sem, out_sem, send_sem, recv_sem, r1_send, r1_recv, r2_send, r2_recv, rf_send, rf_recv, r3_send, r3_recv,
 ):
     row, col = lax.axis_index("row"), lax.axis_index("col")
@@ -297,13 +297,13 @@
 
     def gate_part(lo, hi):
         def body(b, _):
-            i0 = pl.multiple_of(b * 4, 4)
-            normed = norm_rows(zv[pl.ds(i0, 4)].reshape(256, 128), gin, bias_in)
+            i0 = pl.multiple_of(b * 16, 16)
+            normed = norm_rows(zv[pl.ds(i0, 16)].reshape(1024, 128), gin, bias_in)
             g = jax.nn.sigmoid(jnp.dot(normed, wog_ref[...], preferred_element_type=F32))
-            zv[pl.ds(i0, 4)] = g.astype(BF16).reshape(4, 64, 128)
+            zv[pl.ds(i0, 16)] = g.astype(BF16).reshape(16, 64, 128)
             return 0
 
-        lax.fori_loop(lo, hi, body, 0, unroll=4)
+        lax.fori_loop(lo // 4, hi // 4, body, 0)
 
     def prep_right(p):
         ab = p // 2
@@ -347,28 +347,43 @@
             lax.fori_loop(0, 64, pack, 0, unroll=8)
 
     def multiply(h, p):
-        def mul(n, _):
+        def mul(n, total):
             c2 = p * 16 + n
             for cp in range(2):
                 c = (p // 2) * 64 + cp * 32 + (p % 2) * 16 + n
                 part = jnp.dot(r_mat[c2, cp * 64 : cp * 64 + 64, :], lefts[h, c], preferred_element_type=F32)
                 acc[pl.ds(c * 65, 64), :] = part
+                total = total + part
+            return total
+
+        start = jnp.zeros((64, 128), F32) if p == 0 else sums[...]
+        sums[...] = lax.fori_loop(0, 16, mul, start, unroll=8)
+
+    def finish(h):
+        mean = sums[...] * (1.0 / 128)
+
+        def square(c, total):
+            centred = acc[pl.ds(c * 65, 64), :] - mean
+            return total + centred * centred
+
+        spread = lax.fori_loop(0, 128, square, jnp.zeros((64, 128), F32), unroll=8)
+        scale = lax.rsqrt(spread * (1.0 / 128) + 1e-05)
+
+        def normalise(c, _):
+            rows = pl.ds(c * 65, 64)
+            acc[rows, :] = (acc[rows, :] - mean) * scale * gain_c[pl.ds(c, 1), :] + bias_c[pl.ds(c, 1), :]
             return 0
 
-        lax.fori_loop(0, 16, mul, 0, unroll=4)
-
-    def finish(h):
-        def column(j, _):
-            p = acc[pl.ds(j, 128, stride=65), :]
-            mean = jnp.mean(p, axis=0, keepdims=True)
-            centred = p - mean
-            spread = jnp.mean(centred * centred, axis=0, keepdims=True)
-            mixed = centred * lax.rsqrt(spread + 1e-05) * gain_c[...] + bias_c[...]
-            turned = mixed.astype(BF16).T
-            proj[pl.ds(j, 128, stride=65), :] = jnp.dot(turned, wo_ref[...], preferred_element_type=F32)
+        lax.fori_loop(0, 128, normalise, 0, unroll=8)
+
+        def columns(b, _):
+            turned = [acc[pl.ds(b * 4 + n, 128, stride=65), :].astype(BF16).T for n in range(4)]
+            result = jnp.dot(jnp.concatenate(turned, axis=0), wo_ref[...], preferred_element_type=F32)
+            for n in range(4):
+                proj[pl.ds(b * 4 + n, 128, stride=65), :] = result[n * 128 : n * 128 + 128]
             return 0
 
-        lax.fori_loop(0, 64, column, 0, unroll=4)
+        lax.fori_loop(0, 16, columns, 0, unroll=2)
 
         for part in range(4):
             def body(i, _):
@@ -513,6 +528,7 @@
             pltpu.VMEM((2, 128, 192, 128), BF16),
             pltpu.VMEM((2, 64 * 49, 128), F32),
             pltpu.VMEM((128 * 65, 128), F32),
+            pltpu.VMEM((64, 128), F32),
             pltpu.VMEM((128 * 65, 128), F32),
             pltpu.VMEM((128, 128), F32),
             pltpu.VMEM((128, 128), F32),

time: 110 us -> 106 us (0.964)
  Pallas kernels: 105 us -> 100 us
    pallas_call x1, Pallas kernels: 105 us -> 100 us  [body(): pl.pallas_call(kernel, out_shape=jax.ShapeDtypeStruct((256, 64, 128), BF1...]
where the time goes in v2:
time: 106 us; the launch traced here: 105 us
  Pallas kernels  100 us (94%)
  local copies, waits for them, and re-layouts  5.16 us (5%)
    pallas_call x1, Pallas kernels, body(): pl.pallas_call(kernel, out_shape=jax.ShapeDtypeStruct((256, 64, 128), BF1...  100 us
    unnamed x1, local copies, waits for them, and re-layouts  5.16 us

profile of v2, /device:TPU:37, one launch (start us, length us, event | category | flops | bytes accessed | tf_op | source)
XLA Modules:
  0.0 105.5 jit_solution(9294541484944882336)
XLA Ops:
  0.0 100.3 %shard_map.109 = bf16[256,64,128]{2,1,0:T(8,128)(2,1)} custom-call(bf16[256,64,128]{2,1,0:T(8,128)(2,1)} %z_hbm.1, f32[128]{0:T(128)} %gin_ref.1, f32[128]{0:T(128)} %bin_ref.1, bf16[128,128]{1,0:T(8,128)(2,1)} %wlg_ref.1, bf16[128,128]{1,0:T(8,128)(2,1)} %wlp_ref.1, bf16[128,128]{1,0:T(8,128)(2,1)} %wrg_ref.1, bf16[128,128]{1,0:T(8,128)(2,1)} %wrp_ref.1, ...), custom_call_target="tpu_custom_call" | custom-call | flops 2000000000 | bytes 8400000 | tf_op jit(solution)/shard_map/pallas_call | solution.py:513
  100.3 5.2 %copy.13 = bf16[256,64,128]{2,1,0:T(8,128)(2,1)} copy(bf16[256,64,128]{2,1,0:T(8,128)(2,1)} %shard_map.109) | data formatting | bytes 8388608

commit v3 on v2

--- a/solution.py
+++ b/solution.py
@@ -25,7 +25,7 @@
 def kernel(
     z_hbm, gin_ref, bin_ref, wlg_ref, wlp_ref, wrg_ref, wrp_ref, wog_ref, gout_ref, bout_ref, wo_ref,
     out_hbm,
-    zv, zf, wt, normed_w, panel, r_send, r_gather, r_nat, r_mat, lefts, swap, acc, sums, proj, gain_c, bias_c,
+    zv, zf, wt, normed_w, panel, r_send, r_gather, r_nat, r_mat, r_last, lefts, swap, acc, sums, proj, gain_c, bias_c,
     z_sem, out_sem, send_sem, recv_sem, r1_send, r1_recv, r2_send, r2_recv, rf_send, rf_recv, r3_send, r3_recv,
 ):
     row, col = lax.axis_index("row"), lax.axis_index("col")
@@ -308,12 +308,13 @@
     def prep_right(p):
         ab = p // 2
 
-        def relay(s, _):
+        def relay(d, _):
+            s = (second(ab) + d + 3) % 4
             for f in range(4):
                 slot_ = (s * 4 + f) if ab == 0 else (f * 4 + s)
                 for z in range(2):
                     for k in range(NK):
-                        zf[pl.ds(s * 48 + f * 12 + z * NK + k, 16, stride=193), :] = r_nat[
+                        zf[pl.ds(d * 48 + f * 12 + z * NK + k, 16, stride=193), :] = r_nat[
                             z, slot_, k, p * 16 : p * 16 + 16, :
                         ].astype(F32)
             return 0
@@ -321,43 +322,63 @@
         lax.fori_loop(0, 4, relay, 0)
 
         def turn(c, _):
-            m = zf[pl.ds(c * 193, 192), :]
-            r_mat[p * 16 + c] = m.astype(BF16).T
+            r_mat[p * 16 + c] = zf[pl.ds(c * 193, 192), :].astype(BF16).T
+            r_last[p * 16 + c] = zf[pl.ds(c * 193 + 144, 48), :].astype(BF16).T
             return 0
 
         lax.fori_loop(0, 16, turn, 0, unroll=4)
 
+    def spread_rows(h, ab, ds):
+        s = (second(ab) + ds) % 4
+
+        def relay(f, _):
+            for k in range(2 * NK):
+                rows = pl.ds(f * 12 + k, 64, stride=49)
+                swap[ab, rows, :] = panel[h, ab, s * 4 + f, k].astype(F32)
+            return 0
+
+        lax.fori_loop(0, 4, relay, 0)
+
     def relayout(h, ds):
         for ab in range(2):
-            s = (second(ab) + ds) % 4
-
-            def relay(f, _):
-                for k in range(2 * NK):
-                    rows = pl.ds(f * 12 + k, 64, stride=49)
-                    swap[ab, rows, :] = panel[h, ab, s * 4 + f, k].astype(F32)
-                return 0
-
-            lax.fori_loop(0, 4, relay, 0)
+            spread_rows(h, ab, ds)
 
             def pack(c, _):
                 v = swap[ab, pl.ds(c * 49, 48), :]
-                lefts[h, ab * 64 + c, pl.ds(pl.multiple_of(s * 48, 16), 48), :] = v.astype(BF16)
+                lefts[h, ab * 64 + c, (ds + 1) * 48 : (ds + 2) * 48, :] = v.astype(BF16)
                 return 0
 
             lax.fori_loop(0, 64, pack, 0, unroll=8)
 
-    def multiply(h, p):
+    def multiply(h, p, depth):
         def mul(n, total):
             c2 = p * 16 + n
             for cp in range(2):
                 c = (p // 2) * 64 + cp * 32 + (p % 2) * 16 + n
-                part = jnp.dot(r_mat[c2, cp * 64 : cp * 64 + 64, :], lefts[h, c], preferred_element_type=F32)
+                right = r_mat[c2, cp * 64 : cp * 64 + 64, 0:depth]
+                part = jnp.dot(right, lefts[h, c, 0:depth, :], preferred_element_type=F32)
                 acc[pl.ds(c * 65, 64), :] = part
                 total = total + part
             return total
 
         start = jnp.zeros((64, 128), F32) if p == 0 else sums[...]
         sums[...] = lax.fori_loop(0, 16, mul, start, unroll=8)
+
+    def add_last(h):
+        for ab in range(2):
+            spread_rows(h, ab, 2)
+
+            def mul(c2, total):
+                for cp in range(2):
+                    c = cp * 32 + c2
+                    left = swap[ab, pl.ds(c * 49, 48), :].astype(BF16)
+                    right = r_last[ab * 32 + c2, cp * 64 : cp * 64 + 64, :]
+                    part = jnp.dot(right, left, preferred_element_type=F32)
+                    acc[pl.ds((ab * 64 + c) * 65, 64), :] += part
+                    total = total + part
+                return total
+
+            sums[...] = lax.fori_loop(0, 32, mul, sums[...], unroll=8)
 
     def finish(h):
         mean = sums[...] * (1.0 / 128)
@@ -451,26 +472,26 @@
     pass_q1(1, 1)
     wait_right(0)
     prep_right(0)
-    multiply(0, 0)
+    multiply(0, 0, 192)
     wait_right(1)
     prep_right(1)
-    multiply(0, 1)
+    multiply(0, 1, 192)
     relayout(1, 0)
     wait_right(2)
     prep_right(2)
-    multiply(0, 2)
+    multiply(0, 2, 192)
     pass_q1(1, 2)
+    relayout(1, -1)
+    relayout(1, 1)
     wait_right(3)
     prep_right(3)
-    multiply(0, 3)
+    multiply(0, 3, 192)
     finish(0)
-    relayout(1, -1)
-    relayout(1, 1)
+    for p in range(4):
+        multiply(1, p, 144)
     for df in DF:
         wait_q2(1, df)
-    relayout(1, 2)
-    for p in range(4):
-        multiply(1, p)
+    add_last(1)
     finish(1)
 
     for n, c in copies.values():
@@ -507,10 +528,14 @@
             out_copy(h, part).wait()
 
 
+def copy_kernel(x_ref, o_ref):
+    o_ref[...] = x_ref[...]
+
+
 def body(*args):
     vmem = pl.BlockSpec(memory_space=pltpu.VMEM)
     anywhere = pl.BlockSpec(memory_space=pl.ANY)
-    return pl.pallas_call(
+    update = pl.pallas_call(
         kernel,
         out_shape=jax.ShapeDtypeStruct((256, 64, 128), BF16),
         in_specs=[anywhere] + [vmem] * 10,
@@ -525,6 +550,7 @@
             pltpu.VMEM((16, NK, 64, 128), BF16),
             pltpu.VMEM((2, 16, NK, 64, 128), BF16),
             pltpu.VMEM((64, 128, 192), BF16),
+            pltpu.VMEM((64, 128, 48), BF16),
             pltpu.VMEM((2, 128, 192, 128), BF16),
             pltpu.VMEM((2, 64 * 49, 128), F32),
             pltpu.VMEM((128 * 65, 128), F32),
@@ -550,6 +576,16 @@
         ),
         cost_estimate=pl.CostEstimate(flops=2_000_000_000, bytes_accessed=8_400_000, transcendentals=2_000_000),
     )(*args)
+    block = pl.BlockSpec((32, 64, 128), lambda i: (i, 0, 0))
+    return pl.pallas_call(
+        copy_kernel,
+        out_shape=jax.ShapeDtypeStruct((256, 64, 128), BF16),
+        grid=(8,),
+        in_specs=[block],
+        out_specs=block,
+        compiler_params=pltpu.CompilerParams(vmem_limit_bytes=60 * 1024 * 1024),
+        cost_estimate=pl.CostEstimate(flops=0, bytes_accessed=8_400_000, transcendentals=0),
+    )(update)
 
 
 def solution(mesh):

time: 106 us -> 109 us (1.028)
  Pallas kernels: 100 us -> 108 us
  local copies, waits for them, and re-layouts: 5.16 us -> 0 us
    pallas_call x0 -> x1, Pallas kernels: none -> 6.59 us  [body(): pl.pallas_call(copy_kernel, out_shape=jax.ShapeDtypeStruct((256, 64, 128)...]
    unnamed x1 -> x0, local copies, waits for them, and re-layouts: 5.16 us -> none
    pallas_call x1, Pallas kernels: 100 us -> 102 us  [body(): pl.pallas_call(kernel, out_shape=jax.ShapeDtypeStruct((256, 64, 128), BF1...]
where the time goes in v3:
time: 109 us; the launch traced here: 108 us
  Pallas kernels  108 us (99%)
    pallas_call x1, Pallas kernels, body(): pl.pallas_call(kernel, out_shape=jax.ShapeDtypeStruct((256, 64, 128), BF1...  102 us
    pallas_call x1, Pallas kernels, body(): pl.pallas_call(copy_kernel, out_shape=jax.ShapeDtypeStruct((256, 64, 128)...  6.59 us

profile of v3, /device:TPU:37, one launch (start us, length us, event | category | flops | bytes accessed | tf_op | source)
XLA Modules:
  0.0 108.3 jit_solution(199848538309109762)
XLA Ops:
  0.0 101.7 %shard_map.109.x_ref = bf16[256,64,128]{2,1,0:T(8,128)(2,1)} custom-call(bf16[256,64,128]{2,1,0:T(8,128)(2,1)} %z_hbm.1, f32[128]{0:T(128)} %gin_ref.1, f32[128]{0:T(128)} %bin_ref.1, bf16[128,128]{1,0:T(8,128)(2,1)} %wlg_ref.1, bf16[128,128]{1,0:T(8,128)(2,1)} %wlp_ref.1, bf16[128,128]{1,0:T(8,128)(2,1)} %wrg_ref.1, bf16[128,128]{1,0:T(8,128)(2,1)} %wrp_ref.1, ...), custom_call_target="tpu_custom_call" | custom-call | flops 2000000000 | bytes 8400000 | tf_op jit(solution)/shard_map/pallas_call | solution.py:538
  101.7 6.6 %shard_map.110 = bf16[256,64,128]{2,1,0:T(8,128)(2,1)} custom-call(bf16[256,64,128]{2,1,0:T(8,128)(2,1)} %shard_map.109.x_ref), custom_call_target="tpu_custom_call" | custom-call | bytes 8400000 | tf_op jit(solution)/shard_map/pallas_call | solution.py:580

commit v4 on v2

--- a/solution.py
+++ b/solution.py
@@ -1,4 +1,4 @@
-import functools
+from functools import partial
 
 import jax
 import jax.numpy as jnp
@@ -112,20 +112,22 @@
     lax.fori_loop(0, NK, window_right, 0, unroll=3)
     pl.semaphore_wait(barrier, 23)
 
-    count = [0]
     copies = {}
 
     def left_copy(name, ref, target):
-        n = count[0]
-        count[0] += 1
-        c = pltpu.make_async_remote_copy(
-            src_ref=ref, dst_ref=ref, send_sem=send_sem.at[n], recv_sem=recv_sem.at[n], device_id=target, device_id_type=MESH
+        if name not in copies:
+            copies[name] = len(copies), ref, target
+        left_made(name).start()
+
+    def left_made(name):
+        n, ref, target = copies[name]
+        return pltpu.make_async_remote_copy(
+            src_ref=ref(), dst_ref=ref(), send_sem=send_sem.at[n], recv_sem=recv_sem.at[n], device_id=target(),
+            device_id_type=MESH,
         )
-        c.start()
-        copies[name] = (n, c)
 
     def arrived(name, ref):
-        n, _ = copies[name]
+        n = copies[name][0]
         pltpu.make_async_copy(ref, ref, recv_sem.at[n]).wait()
 
     def first(ab):
@@ -151,7 +153,7 @@
 
     def send_z(h):
         for ab in range(2):
-            left_copy(("z", h, ab), z_ref(h, ab, zl), dev(zl_=1 - zl))
+            left_copy(("z", h, ab), partial(z_ref, h, ab, zl), partial(dev, zl_=1 - zl))
 
     def wait_z(h):
         for ab in range(2):
@@ -160,19 +162,19 @@
     def send_p1(h):
         for ab in range(2):
             for d in (1, -1):
-                left_copy(("p1", h, ab, d), pair_ref(h, ab, 0, 0), step_first(ab, d))
+                left_copy(("p1", h, ab, d), partial(pair_ref, h, ab, 0, 0), partial(step_first, ab, d))
 
     def send_q1(h, df):
         for ab in range(2):
             for d in (1, -1):
-                left_copy(("q1", h, ab, df, d), pair_ref(h, ab, 0, df), step_second(ab, d))
+                left_copy(("q1", h, ab, df, d), partial(pair_ref, h, ab, 0, df), partial(step_second, ab, d))
 
     def pass_p1(h):
         for d in (1, -1):
             for ab in range(2):
                 arrived(("p1", h, ab, d), pair_ref(h, ab, 0, -d))
                 half = 0 if d == 1 else 1
-                left_copy(("p2", h, ab, d), pair_ref(h, ab, 0, -d, half), step_first(ab, d))
+                left_copy(("p2", h, ab, d), partial(pair_ref, h, ab, 0, -d, half), partial(step_first, ab, d))
 
     def wait_p2(h):
         for d in (1, -1):
@@ -185,7 +187,7 @@
             for ab in range(2):
                 arrived(("q1", h, ab, df, d), pair_ref(h, ab, -d, df))
                 half = 0 if d == 1 else 1
-                left_copy(("q2", h, ab, df, d), pair_ref(h, ab, -d, df, half), step_second(ab, d))
+                left_copy(("q2", h, ab, df, d), partial(pair_ref, h, ab, -d, df, half), partial(step_second, ab, d))
 
     def wait_q2(h, df):
         for d in (1, -1):
@@ -359,7 +361,7 @@
         start = jnp.zeros((64, 128), F32) if p == 0 else sums[...]
         sums[...] = lax.fori_loop(0, 16, mul, start, unroll=8)
 
-    def finish(h):
+    def normalise_product():
         mean = sums[...] * (1.0 / 128)
 
         def square(c, total):
@@ -376,6 +378,7 @@
 
         lax.fori_loop(0, 128, normalise, 0, unroll=8)
 
+    def finish(h):
         def columns(b, _):
             turned = [acc[pl.ds(b * 4 + n, 128, stride=65), :].astype(BF16).T for n in range(4)]
             result = jnp.dot(jnp.concatenate(turned, axis=0), wo_ref[...], preferred_element_type=F32)
@@ -449,20 +452,28 @@
     pass_r2(3)
     pass_q1(1, -1)
     pass_q1(1, 1)
-    wait_right(0)
-    prep_right(0)
-    multiply(0, 0)
-    wait_right(1)
-    prep_right(1)
-    multiply(0, 1)
+    for p in range(2):
+        wait_right(p)
+        prep_right(p)
+        multiply(0, p)
     relayout(1, 0)
     wait_right(2)
     prep_right(2)
     multiply(0, 2)
-    pass_q1(1, 2)
+
+    @pl.when(rel == 2)
+    def _():
+        pass_q1(1, 2)
+
     wait_right(3)
     prep_right(3)
     multiply(0, 3)
+    normalise_product()
+
+    @pl.when(rel != 2)
+    def _():
+        pass_q1(1, 2)
+
     finish(0)
     relayout(1, -1)
     relayout(1, 1)
@@ -471,10 +482,11 @@
     relayout(1, 2)
     for p in range(4):
         multiply(1, p)
+    normalise_product()
     finish(1)
 
-    for n, c in copies.values():
-        c.wait_send()
+    for name in copies:
+        left_made(name).wait_send()
     for q in range(4):
         @pl.when(jnp.logical_not(r1_mine(q)))
         def _():

time: 106 us -> 106 us (level)
  no operation moved by 1% of the time
where the time goes in v4:
time: 106 us
  Pallas kernels  100 us (94%)
  local copies, waits for them, and re-layouts  5.16 us (5%)
    pallas_call x1, Pallas kernels, body(): pl.pallas_call(kernel, out_shape=jax.ShapeDtypeStruct((256, 64, 128), BF1...  100 us
    unnamed x1, local copies, waits for them, and re-layouts  5.16 us

profile of v4, /device:TPU:37, one launch (start us, length us, event | category | flops | bytes accessed | tf_op | source)
XLA Modules:
  0.0 105.5 jit_solution(12802514475271089560)
XLA Ops:
  0.0 100.4 %shard_map.109 = bf16[256,64,128]{2,1,0:T(8,128)(2,1)} custom-call(bf16[256,64,128]{2,1,0:T(8,128)(2,1)} %z_hbm.1, f32[128]{0:T(128)} %gin_ref.1, f32[128]{0:T(128)} %bin_ref.1, bf16[128,128]{1,0:T(8,128)(2,1)} %wlg_ref.1, bf16[128,128]{1,0:T(8,128)(2,1)} %wlp_ref.1, bf16[128,128]{1,0:T(8,128)(2,1)} %wrg_ref.1, bf16[128,128]{1,0:T(8,128)(2,1)} %wrp_ref.1, ...), custom_call_target="tpu_custom_call" | custom-call | flops 2000000000 | bytes 8400000 | tf_op jit(solution)/shard_map/pallas_call | solution.py:525
  100.4 5.2 %copy.13 = bf16[256,64,128]{2,1,0:T(8,128)(2,1)} copy(bf16[256,64,128]{2,1,0:T(8,128)(2,1)} %shard_map.109) | data formatting | bytes 8388608

commit v5 on v4

--- a/solution.py
+++ b/solution.py
@@ -80,7 +80,7 @@
         normed_w[k] = norm_rows(v, gin, bias_in)
         return 0
 
-    lax.fori_loop(0, NK, norm_window, 0, unroll=3)
+    lax.fori_loop(0, NK, norm_window, 0, unroll=6)
 
     def project(k, part):
         return lax.dot_general(
@@ -109,7 +109,7 @@
                 r_send[2 * u + 1, k, ab * 32 : ab * 32 + 32, :] = jnp.where(low, pltpu.roll(lo, 64, 1), hi).astype(BF16)
         return 0
 
-    lax.fori_loop(0, NK, window_right, 0, unroll=3)
+    lax.fori_loop(0, NK, window_right, 0, unroll=6)
     pl.semaphore_wait(barrier, 23)
 
     copies = {}
@@ -403,7 +403,7 @@
         return pltpu.make_async_copy(zv.at[rows], out_hbm.at[rows], out_sem.at[h * 4 + part])
 
     start_r1()
-    lax.fori_loop(0, NK, window_left, 0, unroll=3)
+    lax.fori_loop(0, NK, window_left, 0, unroll=6)
     send_z(0)
     send_z(1)
     rest.wait()
@@ -446,10 +446,10 @@
     send_q1(1, 2)
     pass_r2(2)
     relayout(0, 1)
+    pass_r2(3)
     for df in DF:
         wait_q2(0, df)
     relayout(0, 2)
-    pass_r2(3)
     pass_q1(1, -1)
     pass_q1(1, 1)
     for p in range(2):

time: 106 us -> 105 us (level); the launches traced: 106 us -> 103 us
  Pallas kernels: 100 us -> 97.4 us
    pallas_call x1, Pallas kernels: 100 us -> 97.4 us  [body(): pl.pallas_call(kernel, out_shape=jax.ShapeDtypeStruct((256, 64, 128), BF1...]
where the time goes in v5:
time: 105 us; the launch traced here: 103 us
  Pallas kernels  97.4 us (93%)
  local copies, waits for them, and re-layouts  5.16 us (5%)
    pallas_call x1, Pallas kernels, body(): pl.pallas_call(kernel, out_shape=jax.ShapeDtypeStruct((256, 64, 128), BF1...  97.4 us
    unnamed x1, local copies, waits for them, and re-layouts  5.16 us

profile of v5, /device:TPU:37, one launch (start us, length us, event | category | flops | bytes accessed | tf_op | source)
XLA Modules:
  0.0 102.6 jit_solution(5816509866696572316)
XLA Ops:
  0.0 97.4 %shard_map.109 = bf16[256,64,128]{2,1,0:T(8,128)(2,1)} custom-call(bf16[256,64,128]{2,1,0:T(8,128)(2,1)} %z_hbm.1, f32[128]{0:T(128)} %gin_ref.1, f32[128]{0:T(128)} %bin_ref.1, bf16[128,128]{1,0:T(8,128)(2,1)} %wlg_ref.1, bf16[128,128]{1,0:T(8,128)(2,1)} %wlp_ref.1, bf16[128,128]{1,0:T(8,128)(2,1)} %wrg_ref.1, bf16[128,128]{1,0:T(8,128)(2,1)} %wrp_ref.1, ...), custom_call_target="tpu_custom_call" | custom-call | flops 2000000000 | bytes 8400000 | tf_op jit(solution)/shard_map/pallas_call | solution.py:525
  97.4 5.2 %copy.13 = bf16[256,64,128]{2,1,0:T(8,128)(2,1)} copy(bf16[256,64,128]{2,1,0:T(8,128)(2,1)} %shard_map.109) | data formatting | bytes 8388608
